TPU v7x, 32 devices: a whole 2x2x4 slice. The times are simulated.
32 devices in a mesh: groups: 2 (over y), ep: 4 (over z), tp: 4 (over x, core).
Axes of the slice: x: 2, y: 2, z: 4, core: 2. Of those that a mesh axis runs over, the one named last changes fastest.
Arguments:
- activations: bfloat16 [1024, 16384], P(('groups', 'ep'), 'tp'), parts along dimension 0, may hold values from -6 to 6
- token_expert_index: int32 [1024, 2], P(('groups', 'ep')), parts along dimension 0, may hold values from 0 to 7, all different within a row; in each aligned block of 128 rows (0 to 127, 128 to 255, ...) at most 40 rows name the same one
- gate_integer_weights: int32 [1024, 2], P(('groups', 'ep')), parts along dimension 0, may hold values from 8192 to 65535
- weight: bfloat16 [8, 16384, 3072], P('ep', 'tp'), may hold values from -2 to 2
- left_reducing_matrices: bfloat16 [8, 16384, 16], P(None, 'tp'), may hold values from -0.046875 to 0.046875
- right_widening_matrices: bfloat16 [8, 16, 3072], P('ep'), may hold values from -0.29882812 to 0.29882812
- magnitude: float32 [8, 3072], P('ep'), may hold values from 0.5 to 2
Outputs:
- projected: bfloat16 [1024, 1, 3072], P(('groups', 'ep'), None, 'tp'), parts along dimension 0
There are 2 independent parts, one for each index of `groups`. A program takes and returns all parts, laid end to end along the dimension named above; an argument that names none is the same for every part. Nothing has to cross between parts.
Inputs may be any that keep to these rules, and one draw needn't show every extreme that they name: `token_expert_index`: the two experts of a token differ. Among the rows of one index of ep no expert is named by more than 40 rows, a bound that some block reaches.
All inputs are finite; a program needn't handle non-finite values.
Results may differ from a plain program's by a relative error of at most 0.014.
Values may be sent and summed in bfloat16 or wider, within the bound.
A program may use at most 128 MiB of HBM per device.

v0:
```python
import jax
import jax.numpy as jnp
from jax import lax
from jax.sharding import PartitionSpec as P

CAP = 40


def column_square_sums(w_block, down_factor_block, b_block):
    merged = w_block.astype(jnp.float32) + 2.0 * jnp.dot(
        down_factor_block, b_block, preferred_element_type=jnp.float32
    )
    return jnp.sum(merged * merged, axis=0)


def on_device(
    activations,
    token_expert_index,
    gate_integer_weights,
    weight,
    left_reducing_matrices,
    right_widening_matrices,
    magnitude,
):
    ep_count = lax.axis_size("ep")
    tok_count = activations.shape[0]
    feat = activations.shape[1]
    units_here = weight.shape[0]
    column_width = weight.shape[2]
    expert_list = left_reducing_matrices.shape[0]
    blocks = units_here * ep_count // expert_list
    flat = token_expert_index.reshape(-1)
    onehot = (flat[:, None] == jnp.arange(expert_list, dtype=jnp.int32)[None, :]).astype(jnp.int32)
    before = jnp.cumsum(onehot, axis=0) - onehot
    slot = jnp.sum(before * onehot, axis=1)
    target = (flat * CAP + slot).reshape(tok_count, 2)
    slot_total = expert_list * CAP
    match = jnp.arange(slot_total, dtype=jnp.int32)[:, None, None] == target[None, :, :]
    placer = jnp.any(match, axis=-1).astype(jnp.bfloat16)
    packed = jnp.dot(placer, activations, preferred_element_type=jnp.float32).astype(jnp.bfloat16)
    copies = jnp.repeat(packed.reshape(expert_list, CAP, feat), blocks, axis=0).reshape(
        ep_count, units_here, CAP, feat
    )
    arrived = lax.all_to_all(copies, "ep", split_axis=0, concat_axis=0, tiled=True)
    first_unit = lax.axis_index("ep") * units_here
    partials = []
    squared_entries = []
    for unit in range(units_here):
        specialist_position = (first_unit + unit) // blocks
        down_factor_block = lax.dynamic_index_in_dim(
            left_reducing_matrices, specialist_position, 0, keepdims=False
        )
        rows = arrived[:, unit].reshape(ep_count * CAP, feat)
        base_output = jnp.dot(rows, weight[unit], preferred_element_type=jnp.float32)
        low_rank_output = jnp.dot(
            rows, down_factor_block, preferred_element_type=jnp.float32
        ).astype(jnp.bfloat16)
        row_totals = base_output + 2.0 * jnp.dot(
            low_rank_output, right_widening_matrices[unit], preferred_element_type=jnp.float32
        )
        partials.append(row_totals.reshape(ep_count, CAP, column_width))
        squared_entries.append(
            column_square_sums(weight[unit], down_factor_block, right_widening_matrices[unit])
        )
    partial_value = jnp.stack(partials, axis=1)
    total_sq = lax.psum(jnp.stack(squared_entries, axis=0), "tp")
    col_scale = magnitude / jnp.sqrt(total_sq + 1e-06)
    gate_real = gate_integer_weights.astype(jnp.float32) / 65536.0
    combiner = jnp.sum(match.astype(jnp.float32) * gate_real[None, :, :], axis=-1).T
    summed = lax.psum_scatter(
        partial_value.astype(jnp.bfloat16), "tp", scatter_dimension=3, tiled=True
    ).astype(jnp.float32)
    width = summed.shape[3]
    scale_part = lax.dynamic_slice_in_dim(col_scale, lax.axis_index("tp") * width, width, 1)
    back = lax.all_to_all(
        (summed * scale_part[None, :, None, :]).astype(jnp.bfloat16),
        "ep",
        split_axis=0,
        concat_axis=0,
        tiled=True,
    ).astype(jnp.float32)
    table = (
        back.reshape(expert_list, blocks, CAP, width)
        .transpose(0, 2, 1, 3)
        .reshape(slot_total, blocks * width)
    )
    mixed = jnp.dot(combiner, table, precision=lax.Precision.HIGHEST).reshape(
        tok_count, blocks, width
    )
    return mixed.astype(jnp.bfloat16)


def solution(mesh):
    return jax.shard_map(
        on_device,
        mesh=mesh,
        in_specs=(
            P(("groups", "ep"), "tp"),
            P(("groups", "ep"), None),
            P(("groups", "ep"), None),
            P("ep", "tp", None),
            P(None, "tp", None),
            P("ep", None, None),
            P("ep", None),
        ),
        out_specs=P(("groups", "ep"), None, "tp"),
        check_vma=False,
    )
```

profile of v0, /device:TPU:0, one launch (start us, length us, event | category | flops | bytes accessed | tf_op | source)
XLA Modules:
  0.0 177.2 jit_solution(13709363941672012718)
XLA Ops:
  6.5 0.0 copy-start
  6.5 0.9 copy.24
  7.4 0.1 eq.43
  7.6 0.1 eq.39
  7.7 0.6 reduce-window.6
  8.3 0.2 slice_reduce_fusion
  8.5 0.1 fusion.33
  8.6 0.1 reduce_sum.39
  8.8 0.1 copy.26
  8.9 0.7 multiply_add_fusion
  9.6 0.0 copy-done
  9.6 2.4 %convolution_convert_fusion = bf16[320,4096]{1,0:T(8,128)(2,1)} fusion(pred[320,128]{1,0:T(8,128)(4,1)S(1)} %fusion.11, bf16[128,4096]{1,0:T(8,128)(2,1)S(1)} %copy-done), kind=kOutput, calls=%fused_computation.8 | convolution fusion | flops 336855040 | bytes 3710976 | tf_op jit(solution)/shard_map/dot_general | solution.py:40
  12.0 6.3 %all-to-all-start = ((bf16[4,2,40,4096]{3,2,1,0:T(8,128)(2,1)}), bf16[4,2,40,4096]{3,2,1,0:T(8,128)(2,1)}, u32[]{:S(2)}, u32[]{:S(2)}) async-start(bf16[4,2,40,4096]{3,2,1,0:T(8,128)(2,1)} %bitcast.60), calls=%async_computation | async-start | bytes 5242880 | tf_op jit(solution)/shard_map/all_to_all | solution.py:44
  18.3 0.0 reduce-scatter.2.cloned.1.call-start
  18.3 59.5 %all-to-all-done = bf16[4,2,40,4096]{3,2,1,0:T(8,128)(2,1)} async-done(((bf16[4,2,40,4096]{3,2,1,0:T(8,128)(2,1)}), bf16[4,2,40,4096]{3,2,1,0:T(8,128)(2,1)}, u32[]{:S(2)}, u32[]{:S(2)}) %all-to-all-start) | async-done | bytes 2621472 | tf_op jit(solution)/shard_map/all_to_all | solution.py:44
  77.8 1.9 %fusion.42 = (bf16[4,1,40,4096]{3,2,1,0:T(8,128)(2,1)S(1)}, bf16[4,1,40,4096]{3,2,1,0:T(8,128)(2,1)S(1)}) fusion(bf16[4,2,40,4096]{3,2,1,0:T(8,128)(2,1)} %all-to-all-done), kind=kLoop, calls=%fused_computation.57 | loop fusion | bytes 5242880 | tf_op jit(solution)/shard_map/slice | solution.py:53
  79.7 0.0 copy-start.2
  79.7 12.1 %fusion = f32[160,3072]{1,0:T(8,128)} fusion(bf16[160,4096]{1,0:T(8,128)(2,1)S(1)} %bitcast.63, bf16[2,4096,3072]{2,1,0:T(8,128)(2,1)} %param.10), kind=kOutput, calls=%fused_computation.2 | convolution fusion | flops 4026531840 | bytes 28442624 | tf_op jit(solution)/shard_map/dot_general | solution.py:54
  91.9 0.0 copy-done.2
  91.9 0.0 copy-start.3
  91.9 11.7 %fusion.2 = f32[160,3072]{1,0:T(8,128)} fusion(bf16[160,4096]{1,0:T(8,128)(2,1)S(1)} %bitcast.61, bf16[2,4096,3072]{2,1,0:T(8,128)(2,1)} %param.10), kind=kOutput, calls=%fused_computation.4 | convolution fusion | flops 4026531840 | bytes 28442624 | tf_op jit(solution)/shard_map/dot_general | solution.py:54
  103.6 0.0 copy-done.3
  103.6 3.4 %fusion.9 = bf16[160,3072]{1,0:T(8,128)(2,1)S(1)} fusion(f32[160,3072]{1,0:T(8,128)} %fusion, bf16[160,4096]{1,0:T(8,128)(2,1)} %bitcast.64, bf16[8,4096,16]{1,2,0:T(8,128)(2,1)} %param.11, s32[]{:T(128)S(6)} %select_n.15, bf16[2,16,3072]{2,1,0:T(8,128)(2,1)S(1)} %copy-done.3), kind=kOutput, calls=%fused_computation.14 | convolution fusion | flops 38177280 | bytes 4489220 | tf_op jit(solution)/shard_map/dot_general | solution.py:58
  107.0 3.0 %fusion.8 = bf16[160,3072]{1,0:T(8,128)(2,1)S(1)} fusion(f32[160,3072]{1,0:T(8,128)} %fusion.2, bf16[160,4096]{1,0:T(8,128)(2,1)S(1)} %bitcast.62, bf16[8,4096,16]{1,2,0:T(8,128)(2,1)} %param.11, s32[]{:T(128)S(6)} %select_n.14, bf16[2,16,3072]{2,1,0:T(8,128)(2,1)S(1)} %copy-done.3), kind=kOutput, calls=%fused_computation.13 | convolution fusion | flops 38177280 | bytes 4489220 | tf_op jit(solution)/shard_map/dot_general | solution.py:58
  110.0 1.5 pad_maximum_fusion
  111.5 0.0 reduce-scatter.2.cloned.1.call-update
  111.5 13.4 %multiply_reduce_fusion = f32[3072]{0:T(1024)S(1)} fusion(bf16[2,4096,3072]{2,1,0:T(8,128)(2,1)} %param.10, bf16[8,4096,16]{1,2,0:T(8,128)(2,1)} %param.11, s32[]{:T(128)S(6)} %select_n.15, bf16[2,16,3072]{2,1,0:T(8,128)(2,1)S(1)} %copy-done.3), kind=kOutput, calls=%fused_computation | convolution fusion | flops 465564672 | bytes 25407492 | tf_op jit(solution)/shard_map/dot_general | solution.py:10
  125.0 0.0 copy-start.1
  125.0 13.4 %multiply_reduce_fusion.1 = f32[3072]{0:T(1024)S(1)} fusion(bf16[2,4096,3072]{2,1,0:T(8,128)(2,1)} %param.10, bf16[8,4096,16]{1,2,0:T(8,128)(2,1)} %param.11, s32[]{:T(128)S(6)} %select_n.14, bf16[2,16,3072]{2,1,0:T(8,128)(2,1)S(1)} %copy-done.3), kind=kOutput, calls=%fused_computation.1 | convolution fusion | flops 465564672 | bytes 25407492 | tf_op jit(solution)/shard_map/dot_general | solution.py:10
  138.4 0.0 copy-start.4
  138.4 10.3 %psum.7 = f32[2,3072]{1,0:T(2,128)S(1)} all-reduce(f32[2,3072]{1,0:T(2,128)S(1)} %pad_maximum_fusion.1), channel_id=1, replica_groups=mesh['groups'=2,'ep'=4,'tp'=4] {'tp'}, use_global_device_ids=true, to_apply=%region_8.9 | all-reduce | flops 6144 | bytes 49152 | tf_op jit(solution)/shard_map/psum | solution.py:66
  148.7 0.7 dynamic-slice_multiply_fusion
  149.4 0.0 reduce-scatter.2.cloned.1.call-done
  149.4 1.9 %multiply_convert_fusion = bf16[4,2,40,768]{3,2,1,0:T(8,128)(2,1)} fusion(bf16[4,2,40,768]{3,2,1,0:T(8,128)(2,1)} %reduce-scatter.2.cloned.1.call-done, f32[2,768]{1,0:T(2,128)S(1)} %dynamic-slice_multiply_fusion), kind=kLoop, calls=%fused_computation.20 | loop fusion | flops 737280 | bytes 989184 | tf_op jit(solution)/shard_map/convert_element_type | solution.py:76
  151.3 3.5 %all-to-all-start.1 = ((bf16[4,2,40,768]{3,2,1,0:T(8,128)(2,1)}), bf16[4,2,40,768]{3,2,1,0:T(8,128)(2,1)S(1)}, u32[]{:S(2)}, u32[]{:S(2)}) async-start(bf16[4,2,40,768]{3,2,1,0:T(8,128)(2,1)} %multiply_convert_fusion), calls=%async_computation.2 | async-start | bytes 983040 | tf_op jit(solution)/shard_map/all_to_all | solution.py:75
  154.8 0.0 copy-done.4
  154.9 14.2 %all-to-all-done.1 = bf16[4,2,40,768]{3,2,1,0:T(8,128)(2,1)S(1)} async-done(((bf16[4,2,40,768]{3,2,1,0:T(8,128)(2,1)}), bf16[4,2,40,768]{3,2,1,0:T(8,128)(2,1)S(1)}, u32[]{:S(2)}, u32[]{:S(2)}) %all-to-all-start.1) | async-done | bytes 491552 | tf_op jit(solution)/shard_map/all_to_all | solution.py:75
  169.1 1.2 fusion.10
  170.3 0.0 copy-done.1
  (7 shorter events, 0.2 us)
Async XLA Ops:
  6.5 3.1 %copy-start = (bf16[128,4096]{1,0:T(8,128)(2,1)S(1)}, bf16[128,4096]{1,0:T(8,128)(2,1)}, u32[]{:S(2)}) copy-start(bf16[128,4096]{1,0:T(8,128)(2,1)} %param.7) | copy-start | bytes 3145732
  12.0 65.9 %all-to-all-start = ((bf16[4,2,40,4096]{3,2,1,0:T(8,128)(2,1)}), bf16[4,2,40,4096]{3,2,1,0:T(8,128)(2,1)}, u32[]{:S(2)}, u32[]{:S(2)}) async-start(bf16[4,2,40,4096]{3,2,1,0:T(8,128)(2,1)} %bitcast.60), calls=%async_computation | async-start | bytes 5242880 | tf_op jit(solution)/shard_map/all_to_all | solution.py:44
  18.3 131.1 %reduce-scatter.2.cloned.1.call-start = ((), (), s32[]{:S(2)}) async-start(), calls=%async_computation.3 | async-start | bytes 2457600 | tf_op jit(solution)/shard_map/reduce_scatter | solution.py:70
  79.7 12.2 %copy-start.2 = (bf16[4,1,40,4096]{3,2,1,0:T(8,128)(2,1)}, bf16[4,1,40,4096]{3,2,1,0:T(8,128)(2,1)S(1)}, u32[]{:S(2)}) copy-start(bf16[4,1,40,4096]{3,2,1,0:T(8,128)(2,1)S(1)} %get-tuple-element.6) | copy-start | bytes 3932164
  91.9 11.7 %copy-start.3 = (bf16[2,16,3072]{2,1,0:T(8,128)(2,1)S(1)}, bf16[2,16,3072]{2,1,0:T(8,128)(2,1)}, u32[]{:S(2)}) copy-start(bf16[2,16,3072]{2,1,0:T(8,128)(2,1)} %param.12) | copy-start | bytes 589828
  125.0 45.4 %copy-start.1 = (bf16[128,4096]{1,0:T(8,128)(2,1)S(1)}, bf16[128,4096]{1,0:T(8,128)(2,1)}, u32[]{:S(2)}) copy-start(bf16[128,4096]{1,0:T(8,128)(2,1)} %param.7) | copy-start | bytes 3145732
  138.4 16.4 %copy-start.4 = (s32[128,2]{0,1:T(2,128)S(1)}, s32[128,2]{0,1:T(2,128)}, u32[]{:S(2)}) copy-start(s32[128,2]{0,1:T(2,128)} %param.9) | copy-start | bytes 3076
  151.3 17.8 %all-to-all-start.1 = ((bf16[4,2,40,768]{3,2,1,0:T(8,128)(2,1)}), bf16[4,2,40,768]{3,2,1,0:T(8,128)(2,1)S(1)}, u32[]{:S(2)}, u32[]{:S(2)}) async-start(bf16[4,2,40,768]{3,2,1,0:T(8,128)(2,1)} %multiply_convert_fusion), calls=%async_computation.2 | async-start | bytes 983040 | tf_op jit(solution)/shard_map/all_to_all | solution.py:75
Sparse Core Ops, SparseCore 0:
  111.6 29.7 reduce-scatter.1
where the time goes:
time: 178 us; the launch traced here: 177 us
  waiting for transfers between devices  73.8 us (41%)
  matrix products  60.7 us (34%)
  between operations  13.5 us (8%)
  blocking collectives  10.3 us (6%)
  starting transfers between devices  9.79 us (5%)
  other arithmetic  5.58 us (3%)
  local copies, waits for them, and re-layouts  3.47 us (2%)
    all_to_all x1, waiting for transfers between devices, on_device(): lax.all_to_all(copies, 'ep', split_axis=0, concat_axis=0, tiled=True)  59.5 us
    dot_general x2, matrix products, column_square_sums(): jnp.dot(down_factor_block, b_block, preferred_element_type=jnp.float32)  26.8 us
    dot_general x2, matrix products, on_device(): jnp.dot(rows, weight[unit], preferred_element_type=jnp.float32)  23.9 us
    all_to_all x1, waiting for transfers between devices, on_device(): lax.all_to_all((summed * scale_part[None, :, None, :]).astype(jnp.bfloat1...  14.2 us
    psum x1, blocking collectives, on_device(): total_sq = lax.psum(jnp.stack(squared_entries, axis=0), 'tp')  10.3 us
    dot_general x2, matrix products, on_device(): jnp.dot(low_rank_output, right_widening_matrices[unit], preferred_element...  6.42 us
    all_to_all x1, starting transfers between devices, on_device(): lax.all_to_all(copies, 'ep', split_axis=0, concat_axis=0, tiled=True)  6.32 us
  transfers between devices with their start and end apart: 3, of which 2 were waited for; matrix products, arithmetic and copies ran while one was open for 16% of the time, Pallas kernels for 0%

commit v1 on v0

v1 whole, which is shorter than its diff:
```python
import functools

import jax
import jax.numpy as jnp
from jax import lax
from jax.experimental import pallas as pl
from jax.experimental.pallas import tpu as pltpu
from jax.sharding import PartitionSpec as P

CAP = 40
KC = 256
TN = 256
NB = 3
LEAD = 3
F32 = jnp.float32
BF16 = jnp.bfloat16


def dispatch_kernel(
    n, units, blocks, rp, nc,
    x_ref, tgt_ref, w_ref, e_ref, b_ref,
    y_ref, sq_ref,
    gath, land, relay, tg, place, lhs, wbuf, acc, low, sqa,
    t_send, t_recv, send, recv, wsem,
):
    me = lax.axis_index("ep")
    tok = x_ref.shape[0]
    width = w_ref.shape[2]
    rank = b_ref.shape[0] // units
    rows = n * rp
    is_end = jnp.logical_or(me == 0, me == n - 1)

    def w_copy(c, u):
        slot = lax.rem(c, NB)
        return pltpu.make_async_copy(
            w_ref.at[u, pl.ds(pl.multiple_of(c * KC, KC), KC), :],
            wbuf.at[slot, pl.ds(u * KC, KC), :],
            wsem.at[slot, u],
        )

    for c in range(min(NB - 1, nc)):
        for u in range(units):
            w_copy(jnp.int32(c), u).start()

    barrier = pltpu.get_barrier_semaphore()

    def greet(d, _):
        pl.semaphore_signal(barrier, inc=1, device_id={"ep": lax.rem(me + d, n)})
        return 0

    lax.fori_loop(1, n, greet, 0)
    pl.semaphore_wait(barrier, n - 1)

    def remote(src, dst, slot, s, c, to):
        return pltpu.make_async_remote_copy(
            src_ref=src, dst_ref=dst, send_sem=send.at[slot, c], recv_sem=recv.at[s, c],
            device_id={"ep": to},
        )

    def own_cols(c):
        return pl.ds(pl.multiple_of(c * KC, KC), KC)

    def own_full(c, slot, to):
        return remote(x_ref.at[:, own_cols(c)], gath.at[me, c], slot, me, c, to)

    def fwd_full(s, c, to):
        return remote(gath.at[s, c], gath.at[s, c], s, s, c, to)

    def packed(s, slot, c, to):
        return remote(relay.at[slot, c], land.at[s, c], slot, s, c, to)

    def pack(role, s, value):
        return jnp.dot(place[role, s], value, preferred_element_type=F32)

    def own_send_full(c):
        @pl.when(me < n - 2)
        def _():
            own_full(c, me, me + 1).start()

        @pl.when(me > 1)
        def _():
            own_full(c, n, me - 1).start()

    def own_send_packed(c):
        @pl.when(me == n - 2)
        def _():
            relay[me, c] = pack(1, me, x_ref[:, own_cols(c)]).astype(BF16)
            packed(me, me, c, n - 1).start()

        @pl.when(me == 1)
        def _():
            relay[n, c] = pack(2, me, x_ref[:, own_cols(c)]).astype(BF16)
            packed(me, n, c, 0).start()

    lead = min(LEAD, nc)

    def tell(to):
        return pltpu.make_async_remote_copy(
            src_ref=tgt_ref, dst_ref=tg.at[me], send_sem=t_send.at[to], recv_sem=t_recv.at[me],
            device_id={"ep": to},
        )

    def hear(s):
        return pltpu.make_async_remote_copy(
            src_ref=tgt_ref, dst_ref=tg.at[s], send_sem=t_send.at[s], recv_sem=t_recv.at[s],
            device_id={"ep": s},
        )

    def start_tell(d, _):
        tell(lax.rem(me + d, n)).start()
        return 0

    lax.fori_loop(1, n, start_tell, 0)
    for c in range(lead):
        own_send_full(jnp.int32(c))
    tg[me] = tgt_ref[...]

    row = lax.broadcasted_iota(jnp.int32, (rp, tok), 0)

    def wanted(dest):
        val = jnp.full((rp, tok), -1, jnp.int32)
        for u in range(units):
            e = (dest * units + u) // blocks
            inside = jnp.logical_and(row >= u * CAP, row < (u + 1) * CAP)
            val = jnp.where(inside, row + (e * CAP - u * CAP), val)
        return val

    def build(s):
        t = tg[s]
        for role, dest in enumerate((me, n - 1, 0)):
            val = wanted(dest)
            hit = jnp.logical_or(t[0:1, :] == val, t[1:2, :] == val)
            place[role, s] = jnp.where(hit, 1.0, 0.0).astype(BF16)

    build(me)
    for c in range(lead):
        own_send_packed(jnp.int32(c))

    acc[...] = jnp.zeros_like(acc)
    low[...] = jnp.zeros_like(low)
    sqa[...] = jnp.zeros_like(sqa)

    def others(d, _):
        s = lax.rem(me + d, n)
        hear(s).wait_recv()
        build(s)
        return 0

    lax.fori_loop(1, n, others, 0)

    mrow = lax.broadcasted_iota(jnp.int32, (rp, KC), 0)

    def put(s, value):
        at = pl.ds(pl.multiple_of(s * rp, 16), rp)
        for u in range(units):
            mine = jnp.logical_and(mrow >= u * CAP, mrow < (u + 1) * CAP)
            lhs[at, pl.ds(u * KC, KC)] = jnp.where(mine, value, 0.0).astype(BF16)

    def arrive(s, c):
        @pl.when(is_end)
        def _():
            packed(s, s, c, s).wait_recv()
            put(s, land[s, c].astype(F32))

        @pl.when(jnp.logical_not(is_end))
        def _():
            fwd_full(s, c, s).wait_recv()

            @pl.when(s < me)
            def _():
                @pl.when(me < n - 2)
                def _():
                    fwd_full(s, c, me + 1).start()

                @pl.when(me == n - 2)
                def _():
                    relay[s, c] = pack(1, s, gath[s, c]).astype(BF16)
                    packed(s, s, c, n - 1).start()

            @pl.when(s > me)
            def _():
                @pl.when(me > 1)
                def _():
                    fwd_full(s, c, me - 1).start()

                @pl.when(me == 1)
                def _():
                    relay[s, c] = pack(2, s, gath[s, c]).astype(BF16)
                    packed(s, s, c, 0).start()

            put(s, pack(0, s, gath[s, c]))

    def step(c, _):
        @pl.when(c + (NB - 1) < nc)
        def _():
            for u in range(units):
                w_copy(c + (NB - 1), u).start()

        @pl.when(c + lead < nc)
        def _():
            own_send_full(c + lead)
            own_send_packed(c + lead)

        def by_distance(d, _):
            @pl.when(me - d >= 0)
            def _():
                arrive(me - d, c)

            @pl.when(me + d < n)
            def _():
                arrive(me + d, c)

            return 0

        lax.fori_loop(1, n, by_distance, 0)
        put(me, pack(0, me, x_ref[:, own_cols(c)]))
        lhs[pl.ds(rows, units * rank), :] = e_ref[c]
        for u in range(units):
            w_copy(c, u).wait()
        slot = lax.rem(c, NB)

        def tile(j, _):
            cols = pl.ds(pl.multiple_of(j * TN, TN), TN)
            acc[:, cols] += jnp.dot(lhs[...], wbuf[slot, :, cols], preferred_element_type=F32)
            for u in range(units):
                w = wbuf[slot, pl.ds(u * KC, KC), cols].astype(F32)
                sqa[u, :, cols] += jnp.sum((w * w).reshape(KC // 8, 8, TN), axis=0)
            return 0

        lax.fori_loop(0, width // TN, tile, 0)
        low[...] += lax.dot_general(
            lhs[...], e_ref[c], (((1,), (1,)), ((), ())), preferred_element_type=F32
        )
        return 0

    lax.fori_loop(0, nc, step, 0)

    low_rows = low[pl.ds(0, rows), :].astype(BF16)
    gram = low[pl.ds(rows, units * rank), :]

    def finish(j, _):
        cols = pl.ds(pl.multiple_of(j * TN, TN), TN)
        b = b_ref[:, cols]
        y_ref[:, cols] = (
            acc[pl.ds(0, rows), cols] + 2.0 * jnp.dot(low_rows, b, preferred_element_type=F32)
        ).astype(BF16)
        bf = b.astype(F32)
        inner = acc[pl.ds(rows, units * rank), cols] + jnp.dot(
            gram, bf, precision=lax.Precision.HIGHEST, preferred_element_type=F32
        )
        cross = bf * inner
        for u in range(units):
            base = jnp.sum(sqa[u, :, cols], axis=0, keepdims=True)
            extra = jnp.sum(cross[u * rank:(u + 1) * rank], axis=0, keepdims=True)
            sq_ref[u:u + 1, cols] = base + 4.0 * extra
        return 0

    lax.fori_loop(0, width // TN, finish, 0)

    def done_tell(d, _):
        tell(lax.rem(me + d, n)).wait_send()
        return 0

    lax.fori_loop(1, n, done_tell, 0)

    def drain(c, _):
        @pl.when(me < n - 2)
        def _():
            own_full(c, me, me + 1).wait_send()

        @pl.when(me == n - 2)
        def _():
            packed(me, me, c, n - 1).wait_send()

        @pl.when(me > 1)
        def _():
            own_full(c, n, me - 1).wait_send()

        @pl.when(me == 1)
        def _():
            packed(me, n, c, 0).wait_send()

        def sent(s, _):
            @pl.when(jnp.logical_and(s < me, me < n - 2))
            def _():
                fwd_full(s, c, me + 1).wait_send()

            @pl.when(jnp.logical_and(s < me, me == n - 2))
            def _():
                packed(s, s, c, n - 1).wait_send()

            @pl.when(jnp.logical_and(s > me, me > 1))
            def _():
                fwd_full(s, c, me - 1).wait_send()

            @pl.when(jnp.logical_and(s > me, me == 1))
            def _():
                packed(s, s, c, 0).wait_send()

            return 0

        @pl.when(jnp.logical_not(is_end))
        def _():
            lax.fori_loop(0, n, sent, 0)

        return 0

    lax.fori_loop(0, nc, drain, 0)


def routed_products(activations, target, weight, mine, widening, n, blocks):
    tok, feat = activations.shape
    units, _, width = weight.shape
    rank = mine.shape[2]
    rp = -(-units * CAP // 16) * 16
    nc = feat // KC
    rows = n * rp
    low_t = mine.reshape(units, nc, KC, rank).transpose(1, 0, 3, 2)
    diag = jnp.eye(units, dtype=BF16)
    e_all = (low_t[:, :, :, None, :] * diag[None, :, None, :, None]).reshape(
        nc, units * rank, units * KC
    )
    b_all = widening.reshape(units * rank, width)
    targets = jnp.pad(target.T, ((0, 6), (0, 0)), constant_values=-2)
    vmem = pl.BlockSpec(memory_space=pltpu.VMEM)
    return pl.pallas_call(
        functools.partial(dispatch_kernel, n, units, blocks, rp, nc),
        out_shape=(
            jax.ShapeDtypeStruct((rows, width), BF16),
            jax.ShapeDtypeStruct((8, width), F32),
        ),
        in_specs=[vmem, vmem, pl.BlockSpec(memory_space=pl.ANY), vmem, vmem],
        out_specs=(vmem, vmem),
        scratch_shapes=[
            pltpu.VMEM((n, nc, tok, KC), BF16),
            pltpu.VMEM((n, nc, rp, KC), BF16),
            pltpu.VMEM((n + 1, nc, rp, KC), BF16),
            pltpu.VMEM((n, 8, tok), jnp.int32),
            pltpu.VMEM((3, n, rp, tok), BF16),
            pltpu.VMEM((rows + units * rank, units * KC), BF16),
            pltpu.VMEM((NB, units * KC, width), BF16),
            pltpu.VMEM((rows + units * rank, width), F32),
            pltpu.VMEM((rows + units * rank, units * rank), F32),
            pltpu.VMEM((units, 8, width), F32),
            pltpu.SemaphoreType.DMA((n,)),
            pltpu.SemaphoreType.DMA((n,)),
            pltpu.SemaphoreType.DMA((n + 1, nc)),
            pltpu.SemaphoreType.DMA((n, nc)),
            pltpu.SemaphoreType.DMA((NB, units)),
        ],
        compiler_params=pltpu.CompilerParams(
            collective_id=0, has_side_effects=True, vmem_limit_bytes=60 * 1024 * 1024
        ),
        cost_estimate=pl.CostEstimate(
            flops=2 * rows * feat * width, bytes_accessed=2 * units * feat * width, transcendentals=0
        ),
        name="routed_products",
    )(activations, targets, weight, e_all, b_all)


def on_device(
    activations,
    token_expert_index,
    gate_integer_weights,
    weight,
    left_reducing_matrices,
    right_widening_matrices,
    magnitude,
):
    ep_count = lax.axis_size("ep")
    tok_count = activations.shape[0]
    units_here = weight.shape[0]
    expert_list = left_reducing_matrices.shape[0]
    blocks = units_here * ep_count // expert_list
    flat = token_expert_index.reshape(-1)
    onehot = (flat[:, None] == jnp.arange(expert_list, dtype=jnp.int32)[None, :]).astype(jnp.int32)
    before = jnp.cumsum(onehot, axis=0) - onehot
    slot = jnp.sum(before * onehot, axis=1)
    target = (flat * CAP + slot).reshape(tok_count, 2)
    slot_total = expert_list * CAP
    match = jnp.arange(slot_total, dtype=jnp.int32)[:, None, None] == target[None, :, :]
    first_unit = lax.axis_index("ep") * units_here
    mine = jnp.stack(
        [
            lax.dynamic_index_in_dim(
                left_reducing_matrices, (first_unit + unit) // blocks, 0, keepdims=False
            )
            for unit in range(units_here)
        ],
        axis=0,
    )
    partial_rows, squares = routed_products(
        activations, target, weight, mine, right_widening_matrices, ep_count, blocks
    )
    total_sq = jnp.maximum(lax.psum(squares[:units_here], "tp"), 0.0)
    col_scale = magnitude / jnp.sqrt(total_sq + 1e-06)
    gate_real = gate_integer_weights.astype(F32) / 65536.0
    combiner = jnp.sum(match.astype(F32) * gate_real[None, :, :], axis=-1).T
    summed = lax.psum_scatter(partial_rows, "tp", scatter_dimension=1, tiled=True).astype(F32)
    width = summed.shape[1]
    summed = summed.reshape(ep_count, -1, width)[:, : units_here * CAP].reshape(
        ep_count, units_here, CAP, width
    )
    scale_part = lax.dynamic_slice_in_dim(col_scale, lax.axis_index("tp") * width, width, 1)
    back = lax.all_to_all(
        (summed * scale_part[None, :, None, :]).astype(BF16),
        "ep",
        split_axis=0,
        concat_axis=0,
        tiled=True,
    ).astype(F32)
    table = (
        back.reshape(expert_list, blocks, CAP, width)
        .transpose(0, 2, 1, 3)
        .reshape(slot_total, blocks * width)
    )
    mixed = jnp.dot(combiner, table, precision=lax.Precision.HIGHEST).reshape(
        tok_count, blocks, width
    )
    return mixed.astype(BF16)


def solution(mesh):
    return jax.shard_map(
        on_device,
        mesh=mesh,
        in_specs=(
            P(("groups", "ep"), "tp"),
            P(("groups", "ep"), None),
            P(("groups", "ep"), None),
            P("ep", "tp", None),
            P(None, "tp", None),
            P("ep", None, None),
            P("ep", None),
        ),
        out_specs=P(("groups", "ep"), None, "tp"),
        check_vma=False,
    )
```

time: 178 us -> 217 us (1.22)
  Pallas kernels: 0 us -> 146 us
  matrix products: 60.7 us -> 1.23 us
  waiting for transfers between devices: 73.8 us -> 30.9 us
  starting transfers between devices: 9.79 us -> 4.62 us
    pallas_call x0 -> x1, Pallas kernels: none -> 146 us  [routed_products(): pl.pallas_call(functools.partial(dispatch_kernel, n, units, blocks, rp, n...]
    all_to_all x2 -> x1, waiting for transfers between devices: 73.8 us -> 13.7 us  [on_device(): lax.all_to_all((summed * scale_part[None, :, None, :]).astype(BF16), 'ep'...]
    dot_general x7 -> x0, matrix products: 59.5 us -> none  [the longest x2 26.8 us: column_square_sums(): jnp.dot(down_factor_block, b_block, preferred_element_type=jnp.float32)]
    reduce_scatter x1, waiting for transfers between devices: 0.02 us -> 17.1 us  [on_device(): lax.psum_scatter(partial_rows, 'tp', scatter_dimension=1, tiled=True)]
    all_to_all x2 -> x1, starting transfers between devices: 9.78 us -> 4.62 us  [on_device(): lax.all_to_all((summed * scale_part[None, :, None, :]).astype(BF16), 'ep'...]
  transfers between devices with their start and end apart: 3 -> 2, of which waited for: 2 -> 2; matrix products, arithmetic and copies ran while one was open for 16% -> 1% of each run, Pallas kernels for 0% -> 0%
where the time goes in v1:
time: 217 us
  Pallas kernels  146 us (67%)
  waiting for transfers between devices  30.9 us (14%)
  between operations  13.5 us (6%)
  blocking collectives  10.3 us (5%)
  local copies, waits for them, and re-layouts  5 us (2%)
  other arithmetic  4.93 us (2%)
  starting transfers between devices  4.62 us (2%)
    pallas_call x1, Pallas kernels, routed_products(): pl.pallas_call(functools.partial(dispatch_kernel, n, units, blocks, rp, n...  146 us
    reduce_scatter x1, waiting for transfers between devices, on_device(): lax.psum_scatter(partial_rows, 'tp', scatter_dimension=1, tiled=True)  17.1 us
    all_to_all x1, waiting for transfers between devices, on_device(): lax.all_to_all((summed * scale_part[None, :, None, :]).astype(BF16), 'ep'...  13.7 us
    psum x1, blocking collectives, on_device(): total_sq = jnp.maximum(lax.psum(squares[:units_here], 'tp'), 0.0)  10.3 us
    all_to_all x1, starting transfers between devices, on_device(): lax.all_to_all((summed * scale_part[None, :, None, :]).astype(BF16), 'ep'...  4.62 us
  transfers between devices with their start and end apart: 2, of which 2 were waited for; matrix products, arithmetic and copies ran while one was open for 1% of the time, Pallas kernels for 0%

profile of v1, /device:TPU:0, one launch (start us, length us, event | category | flops | bytes accessed | tf_op | source)
XLA Modules:
  0.0 216.5 jit_solution(14823033660433335301)
XLA Ops:
  6.5 0.0 copy-start
  6.5 0.0 reduce-scatter.2.cloned.1.call-start
  6.5 0.8 copy.17
  7.3 0.1 eq.50
  7.5 0.1 eq.46
  7.6 1.0 constant_dynamic-slice_fusion.1
  8.7 0.1 copy.20
  8.8 0.5 mul.60
  9.3 0.3 mul.61
  9.6 0.1 mul.62
  9.7 0.6 reduce-window.6
  10.3 0.2 slice_reduce_fusion
  10.6 0.1 fusion.3
  10.7 0.1 reduce_sum.21
  10.8 0.1 copy.19
  10.9 0.7 multiply_add_fusion
  11.6 0.8 broadcast_multiply_fusion.e_ref
  12.4 0.6 pad.4.tgt_ref
  13.0 146.1 %routed_products.1 = (bf16[320,3072]{1,0:T(8,128)(2,1)}, f32[8,3072]{1,0:T(8,128)}) custom-call(bf16[128,4096]{1,0:T(8,128)(2,1)} %x_ref.1, s32[8,128]{1,0:T(8,128)} %pad.4.tgt_ref, bf16[2,4096,3072]{2,1,0:T(8,128)(2,1)} %w_ref.1, bf16[16,32,512]{2,1,0:T(8,128)(2,1)} %broadcast_multiply_fusion.e_ref, bf16[32,3072]{1,0:T(8,128)(2,1)} %bitcast.32), custom_call_target="tpu_custom_call" | custom-call | flops 8053063680 | bytes 50331648 | tf_op jit(solution)/shard_map/routed_products/pallas_call | solution.py:326
  159.2 0.0 reduce-scatter.2.cloned.1.call-update
  159.2 0.9 slice.11
  160.1 10.3 %psum.7 = f32[2,3072]{1,0:T(2,128)S(1)} all-reduce(f32[2,3072]{1,0:T(2,128)S(1)} %slice.11), channel_id=1, replica_groups=mesh['groups'=2,'ep'=4,'tp'=4] {'tp'}, use_global_device_ids=true, to_apply=%region_5.6 | all-reduce | flops 6144 | bytes 49152 | tf_op jit(solution)/shard_map/psum | solution.py:395
  170.3 0.7 dynamic-slice_multiply_fusion
  171.0 17.1 %reduce-scatter.2.cloned.1.call-done = bf16[320,768]{1,0:T(8,128)(2,1)} async-done(((bf16[320,3072]{1,0:T(8,128)(2,1)}), bf16[320,768]{1,0:T(8,128)(2,1)}) %reduce-scatter.2.cloned.1.call-update) | async-done | bytes 491536 | tf_op jit(solution)/shard_map/reduce_scatter | solution.py:399
  188.2 1.9 fusion.1
  190.0 4.6 %all-to-all-start = ((bf16[4,2,40,768]{3,2,1,0:T(8,128)(2,1)}), bf16[4,2,40,768]{3,2,1,0:T(8,128)(2,1)S(1)}, u32[]{:S(2)}, u32[]{:S(2)}) async-start(bf16[4,2,40,768]{3,2,1,0:T(8,128)(2,1)} %fusion.1), calls=%async_computation.1 | async-start | bytes 983040 | tf_op jit(solution)/shard_map/all_to_all | solution.py:405
  194.7 0.0 copy-done
  194.7 13.7 %all-to-all-done = bf16[4,2,40,768]{3,2,1,0:T(8,128)(2,1)S(1)} async-done(((bf16[4,2,40,768]{3,2,1,0:T(8,128)(2,1)}), bf16[4,2,40,768]{3,2,1,0:T(8,128)(2,1)S(1)}, u32[]{:S(2)}, u32[]{:S(2)}) %all-to-all-start) | async-done | bytes 491552 | tf_op jit(solution)/shard_map/all_to_all | solution.py:405
  208.5 1.2 fusion
  (9 shorter events, 0.2 us)
Async XLA Ops:
  6.5 188.1 %copy-start = (s32[128,2]{0,1:T(2,128)S(1)}, s32[128,2]{0,1:T(2,128)}, u32[]{:S(2)}) copy-start(s32[128,2]{0,1:T(2,128)} %param.9) | copy-start | bytes 3076
  6.5 181.6 %reduce-scatter.2.cloned.1.call-start = ((), (), s32[]{:S(2)}) async-start(), calls=%async_computation.2 | async-start | bytes 2457600 | tf_op jit(solution)/shard_map/reduce_scatter | solution.py:399
  190.0 18.4 %all-to-all-start = ((bf16[4,2,40,768]{3,2,1,0:T(8,128)(2,1)}), bf16[4,2,40,768]{3,2,1,0:T(8,128)(2,1)S(1)}, u32[]{:S(2)}, u32[]{:S(2)}) async-start(bf16[4,2,40,768]{3,2,1,0:T(8,128)(2,1)} %fusion.1), calls=%async_computation.1 | async-start | bytes 983040 | tf_op jit(solution)/shard_map/all_to_all | solution.py:405
Sparse Core Ops, SparseCore 0:
  159.3 28.8 reduce-scatter.1

commit v2 on v1

--- a/solution.py
+++ b/solution.py
@@ -8,22 +8,30 @@
 from jax.sharding import PartitionSpec as P
 
 CAP = 40
-KC = 256
-TN = 256
+KC = 512
 NB = 3
-LEAD = 3
+GAP = 1
 F32 = jnp.float32
 BF16 = jnp.bfloat16
 
 
 def dispatch_kernel(
-    n, units, blocks, rp, nc,
-    x_ref, tgt_ref, w_ref, e_ref, b_ref,
-    y_ref, sq_ref,
-    gath, land, relay, tg, place, lhs, wbuf, acc, low, sqa,
-    t_send, t_recv, send, recv, wsem,
+    n, tp, units, blocks, rp, nc, tn, fused,
+    *refs,
 ):
+    x_ref, tgt_ref, w_ref, e_ref, b_ref = refs[:5]
+    if fused:
+        mag_ref, hi_ref, lo_ref, out_ref = refs[5:9]
+        refs, tail = refs[9:28], refs[28:]
+    else:
+        y_ref, sq_ref = refs[5:7]
+        refs = refs[7:26]
+    (
+        gath, land, relay, tg, place, lhs, wbuf, acc, low, sqa, sqs, sqr,
+        t_send, t_recv, send, recv, wsem, q_send, q_recv,
+    ) = refs
     me = lax.axis_index("ep")
+    mt = lax.axis_index("tp")
     tok = x_ref.shape[0]
     width = w_ref.shape[2]
     rank = b_ref.shape[0] // units
@@ -48,8 +56,13 @@
         pl.semaphore_signal(barrier, inc=1, device_id={"ep": lax.rem(me + d, n)})
         return 0
 
+    def greet_tp(d, _):
+        pl.semaphore_signal(barrier, inc=1, device_id={"tp": lax.rem(mt + d, tp)})
+        return 0
+
     lax.fori_loop(1, n, greet, 0)
-    pl.semaphore_wait(barrier, n - 1)
+    lax.fori_loop(1, tp, greet_tp, 0)
+    pl.semaphore_wait(barrier, n + tp - 2)
 
     def remote(src, dst, slot, s, c, to):
         return pltpu.make_async_remote_copy(
@@ -92,8 +105,6 @@
             relay[n, c] = pack(2, me, x_ref[:, own_cols(c)]).astype(BF16)
             packed(me, n, c, 0).start()
 
-    lead = min(LEAD, nc)
-
     def tell(to):
         return pltpu.make_async_remote_copy(
             src_ref=tgt_ref, dst_ref=tg.at[me], send_sem=t_send.at[to], recv_sem=t_recv.at[me],
@@ -111,8 +122,12 @@
         return 0
 
     lax.fori_loop(1, n, start_tell, 0)
-    for c in range(lead):
-        own_send_full(jnp.int32(c))
+
+    def own_all(c, _):
+        own_send_full(c)
+        return 0
+
+    lax.fori_loop(0, nc, own_all, 0)
     tg[me] = tgt_ref[...]
 
     row = lax.broadcasted_iota(jnp.int32, (rp, tok), 0)
@@ -133,8 +148,12 @@
             place[role, s] = jnp.where(hit, 1.0, 0.0).astype(BF16)
 
     build(me)
-    for c in range(lead):
-        own_send_packed(jnp.int32(c))
+
+    def own_all_packed(c, _):
+        own_send_packed(c)
+        return 0
+
+    lax.fori_loop(0, nc, own_all_packed, 0)
 
     acc[...] = jnp.zeros_like(acc)
     low[...] = jnp.zeros_like(low)
@@ -160,7 +179,6 @@
         @pl.when(is_end)
         def _():
             packed(s, s, c, s).wait_recv()
-            put(s, land[s, c].astype(F32))
 
         @pl.when(jnp.logical_not(is_end))
         def _():
@@ -188,7 +206,28 @@
                     relay[s, c] = pack(2, s, gath[s, c]).astype(BF16)
                     packed(s, s, c, 0).start()
 
-            put(s, pack(0, s, gath[s, c]))
+    def arrivals(c):
+        def by_distance(d, _):
+            k = c + (n - 1 - d) * GAP
+            live = jnp.logical_and(k >= 0, k < nc)
+
+            @pl.when(jnp.logical_and(live, me - d >= 0))
+            def _():
+                arrive(me - d, k)
+
+            @pl.when(jnp.logical_and(live, me + d < n))
+            def _():
+                arrive(me + d, k)
+
+            return 0
+
+        lax.fori_loop(1, n, by_distance, 0)
+
+    def early(i, _):
+        arrivals(i - (n - 2) * GAP)
+        return 0
+
+    lax.fori_loop(0, (n - 2) * GAP, early, 0)
 
     def step(c, _):
         @pl.when(c + (NB - 1) < nc)
@@ -196,23 +235,22 @@
             for u in range(units):
                 w_copy(c + (NB - 1), u).start()
 
-        @pl.when(c + lead < nc)
-        def _():
-            own_send_full(c + lead)
-            own_send_packed(c + lead)
-
-        def by_distance(d, _):
-            @pl.when(me - d >= 0)
-            def _():
-                arrive(me - d, c)
-
-            @pl.when(me + d < n)
-            def _():
-                arrive(me + d, c)
+        arrivals(c)
+
+        def gather_row(d, _):
+            s = lax.rem(me + d, n)
+
+            @pl.when(is_end)
+            def _():
+                put(s, land[s, c].astype(F32))
+
+            @pl.when(jnp.logical_not(is_end))
+            def _():
+                put(s, pack(0, s, gath[s, c]))
 
             return 0
 
-        lax.fori_loop(1, n, by_distance, 0)
+        lax.fori_loop(1, n, gather_row, 0)
         put(me, pack(0, me, x_ref[:, own_cols(c)]))
         lhs[pl.ds(rows, units * rank), :] = e_ref[c]
         for u in range(units):
@@ -220,14 +258,14 @@
         slot = lax.rem(c, NB)
 
         def tile(j, _):
-            cols = pl.ds(pl.multiple_of(j * TN, TN), TN)
+            cols = pl.ds(pl.multiple_of(j * tn, tn), tn)
             acc[:, cols] += jnp.dot(lhs[...], wbuf[slot, :, cols], preferred_element_type=F32)
             for u in range(units):
                 w = wbuf[slot, pl.ds(u * KC, KC), cols].astype(F32)
-                sqa[u, :, cols] += jnp.sum((w * w).reshape(KC // 8, 8, TN), axis=0)
+                sqa[u, :, cols] += jnp.sum((w * w).reshape(KC // 8, 8, tn), axis=0)
             return 0
 
-        lax.fori_loop(0, width // TN, tile, 0)
+        lax.fori_loop(0, width // tn, tile, 0)
         low[...] += lax.dot_general(
             lhs[...], e_ref[c], (((1,), (1,)), ((), ())), preferred_element_type=F32
         )
@@ -238,13 +276,9 @@
     low_rows = low[pl.ds(0, rows), :].astype(BF16)
     gram = low[pl.ds(rows, units * rank), :]
 
-    def finish(j, _):
-        cols = pl.ds(pl.multiple_of(j * TN, TN), TN)
-        b = b_ref[:, cols]
-        y_ref[:, cols] = (
-            acc[pl.ds(0, rows), cols] + 2.0 * jnp.dot(low_rows, b, preferred_element_type=F32)
-        ).astype(BF16)
-        bf = b.astype(F32)
+    def squares(j, _):
+        cols = pl.ds(pl.multiple_of(j * tn, tn), tn)
+        bf = b_ref[:, cols].astype(F32)
         inner = acc[pl.ds(rows, units * rank), cols] + jnp.dot(
             gram, bf, precision=lax.Precision.HIGHEST, preferred_element_type=F32
         )
@@ -252,10 +286,139 @@
         for u in range(units):
             base = jnp.sum(sqa[u, :, cols], axis=0, keepdims=True)
             extra = jnp.sum(cross[u * rank:(u + 1) * rank], axis=0, keepdims=True)
-            sq_ref[u:u + 1, cols] = base + 4.0 * extra
-        return 0
-
-    lax.fori_loop(0, width // TN, finish, 0)
+            sqs[u:u + 1, cols] = base + 4.0 * extra
+        return 0
+
+    sqs[...] = jnp.zeros_like(sqs)
+    lax.fori_loop(0, width // tn, squares, 0)
+
+    def square_copy(d):
+        return pltpu.make_async_remote_copy(
+            src_ref=sqs, dst_ref=sqr.at[d], send_sem=q_send.at[d], recv_sem=q_recv.at[d],
+            device_id={"tp": lax.rem(mt + d, tp)},
+        )
+
+    for d in range(1, tp):
+        square_copy(d).start()
+
+    if not fused:
+
+        def finish(j, _):
+            cols = pl.ds(pl.multiple_of(j * tn, tn), tn)
+            y_ref[:, cols] = (
+                acc[pl.ds(0, rows), cols]
+                + 2.0 * jnp.dot(low_rows, b_ref[:, cols], preferred_element_type=F32)
+            ).astype(BF16)
+            return 0
+
+        lax.fori_loop(0, width // tn, finish, 0)
+        for d in range(1, tp):
+            square_copy(d).wait_recv()
+        total = sqs[...]
+        for d in range(1, tp):
+            total = total + sqr[d]
+        sq_ref[...] = total
+    else:
+        ys, got1, half, got2, outgo, back, s1, r1, s2, r2, s3, r3 = tail
+        wp = width // tp
+        pairs = tp // 2
+        core = lax.rem(mt, 2)
+        mx = mt // 2
+        other = 1 - core
+
+        def make_part(p):
+            cols = pl.ds(pl.multiple_of(p * wp, 128), wp)
+            ys[p] = (
+                acc[pl.ds(0, rows), cols]
+                + 2.0 * jnp.dot(low_rows, b_ref[:, cols], preferred_element_type=F32)
+            ).astype(BF16)
+
+        def to_core(i):
+            return pltpu.make_async_remote_copy(
+                src_ref=ys.at[2 * i + other], dst_ref=got1.at[i], send_sem=s1.at[i], recv_sem=r1.at[i],
+                device_id={"tp": 2 * mx + other},
+            )
+
+        order = [lax.rem(mx + 1 + i, pairs) for i in range(pairs)]
+        for i in order:
+            make_part(2 * i + other)
+            to_core(i).start()
+        for i in order:
+            make_part(2 * i + core)
+
+        def span(blk):
+            return pl.ds(pl.multiple_of(blk * rp, 16), rp)
+
+        def to_chip(i, k, blk):
+            return pltpu.make_async_remote_copy(
+                src_ref=half.at[i, span(blk)], dst_ref=got2.at[k, span(blk)],
+                send_sem=s2.at[k, blk], recv_sem=r2.at[k, blk],
+                device_id={"tp": 2 * i + core},
+            )
+
+        turns = [lax.rem(me + 1 + i, n) for i in range(n)]
+        for k, i in enumerate(order[:-1]):
+            to_core(i).wait_recv()
+            for blk in turns:
+                half[i, span(blk)] = (
+                    ys[2 * i + core, span(blk)].astype(F32) + got1[i, span(blk)].astype(F32)
+                ).astype(BF16)
+                to_chip(i, k, blk).start()
+        to_core(mx).wait_recv()
+        for d in range(1, tp):
+            square_copy(d).wait_recv()
+        mycols = pl.ds(pl.multiple_of(mt * wp, 128), wp)
+        total = sqs[:, mycols]
+        for d in range(1, tp):
+            total = total + sqr[d, :, mycols]
+        total = jnp.maximum(total[:units], 0.0)
+        col_scale = mag_ref[:, mycols] / jnp.sqrt(total + 1e-06)
+        orow = lax.broadcasted_iota(jnp.int32, (rp, wp), 0)
+        row_scale = jnp.zeros((rp, wp), F32)
+        for u in range(units):
+            inside = jnp.logical_and(orow >= u * CAP, orow < (u + 1) * CAP)
+            row_scale = jnp.where(inside, col_scale[u:u + 1], row_scale)
+
+        def home(blk):
+            return pltpu.make_async_remote_copy(
+                src_ref=outgo.at[blk], dst_ref=back.at[me], send_sem=s3.at[blk], recv_sem=r3.at[me],
+                device_id={"ep": blk},
+            )
+
+        def landed(src):
+            return pltpu.make_async_remote_copy(
+                src_ref=outgo.at[src], dst_ref=back.at[src], send_sem=s3.at[src], recv_sem=r3.at[src],
+                device_id={"ep": src},
+            )
+
+        for t, blk in enumerate(turns):
+            value = ys[mt, span(blk)].astype(F32) + got1[mx, span(blk)].astype(F32)
+            for k, i in enumerate(order[:-1]):
+                to_chip(i, k, blk).wait_recv()
+                value = value + got2[k, span(blk)].astype(F32)
+            value = (value * row_scale).astype(BF16)
+            if t < n - 1:
+                outgo[blk] = value
+                home(blk).start()
+            else:
+                back[me] = value
+        for i in turns[:-1]:
+            landed(i).wait_recv()
+        table = back[...].reshape(rows, wp)
+        out_ref[...] = (
+            jnp.dot(hi_ref[...], table, preferred_element_type=F32)
+            + jnp.dot(lo_ref[...], table, preferred_element_type=F32)
+        ).astype(BF16)
+        for i in turns[:-1]:
+            home(i).wait_send()
+        for i in order:
+            to_core(i).wait_send()
+        for k, i in enumerate(order[:-1]):
+            for blk in turns:
+                to_chip(i, k, blk).wait_send()
+
+    for d in range(1, tp):
+        square_copy(d).wait_send()
 
     def done_tell(d, _):
         tell(lax.rem(me + d, n)).wait_send()
@@ -308,12 +471,14 @@
     lax.fori_loop(0, nc, drain, 0)
 
 
-def routed_products(activations, target, weight, mine, widening, n, blocks):
+def routed_products(activations, target, weight, mine, widening, n, blocks, tail_in):
     tok, feat = activations.shape
     units, _, width = weight.shape
     rank = mine.shape[2]
     rp = -(-units * CAP // 16) * 16
     nc = feat // KC
+    tp = lax.axis_size("tp")
+    tn = width // 3 if width % 384 == 0 else width
     rows = n * rp
     low_t = mine.reshape(units, nc, KC, rank).transpose(1, 0, 3, 2)
     diag = jnp.eye(units, dtype=BF16)
@@ -323,14 +488,38 @@
     b_all = widening.reshape(units * rank, width)
     targets = jnp.pad(target.T, ((0, 6), (0, 0)), constant_values=-2)
     vmem = pl.BlockSpec(memory_space=pltpu.VMEM)
-    return pl.pallas_call(
-        functools.partial(dispatch_kernel, n, units, blocks, rp, nc),
-        out_shape=(
+    wp = width // tp
+    fused = len(tail_in) > 0
+    if fused:
+        out_shape = jax.ShapeDtypeStruct((tok, wp), BF16)
+        out_specs = vmem
+        tail_scratch = [
+            pltpu.VMEM((tp, rows, wp), BF16),
+            pltpu.VMEM((tp // 2, rows, wp), BF16),
+            pltpu.VMEM((tp // 2, rows, wp), BF16),
+            pltpu.VMEM((tp // 2, rows, wp), BF16),
+            pltpu.VMEM((n, rp, wp), BF16),
+            pltpu.VMEM((n, rp, wp), BF16),
+            pltpu.SemaphoreType.DMA((tp // 2,)),
+            pltpu.SemaphoreType.DMA((tp // 2,)),
+            pltpu.SemaphoreType.DMA((tp // 2, n)),
+            pltpu.SemaphoreType.DMA((tp // 2, n)),
+            pltpu.SemaphoreType.DMA((n,)),
+            pltpu.SemaphoreType.DMA((n,)),
+        ]
+    else:
+        out_shape = (
             jax.ShapeDtypeStruct((rows, width), BF16),
             jax.ShapeDtypeStruct((8, width), F32),
-        ),
-        in_specs=[vmem, vmem, pl.BlockSpec(memory_space=pl.ANY), vmem, vmem],
-        out_specs=(vmem, vmem),
+        )
+        out_specs = (vmem, vmem)
+        tail_scratch = []
+    return pl.pallas_call(
+        functools.partial(dispatch_kernel, n, tp, units, blocks, rp, nc, tn, fused),
+        out_shape=out_shape,
+        in_specs=[vmem, vmem, pl.BlockSpec(memory_space=pl.ANY), vmem, vmem]
+        + [vmem] * len(tail_in),
+        out_specs=out_specs,
         scratch_shapes=[
             pltpu.VMEM((n, nc, tok, KC), BF16),
             pltpu.VMEM((n, nc, rp, KC), BF16),
@@ -342,12 +531,17 @@
             pltpu.VMEM((rows + units * rank, width), F32),
             pltpu.VMEM((rows + units * rank, units * rank), F32),
             pltpu.VMEM((units, 8, width), F32),
+            pltpu.VMEM((8, width), F32),
+            pltpu.VMEM((tp, 8, width), F32),
             pltpu.SemaphoreType.DMA((n,)),
             pltpu.SemaphoreType.DMA((n,)),
             pltpu.SemaphoreType.DMA((n + 1, nc)),
             pltpu.SemaphoreType.DMA((n, nc)),
             pltpu.SemaphoreType.DMA((NB, units)),
-        ],
+            pltpu.SemaphoreType.DMA((tp,)),
+            pltpu.SemaphoreType.DMA((tp,)),
+        ]
+        + tail_scratch,
         compiler_params=pltpu.CompilerParams(
             collective_id=0, has_side_effects=True, vmem_limit_bytes=60 * 1024 * 1024
         ),
@@ -355,7 +549,7 @@
             flops=2 * rows * feat * width, bytes_accessed=2 * units * feat * width, transcendentals=0
         ),
         name="routed_products",
-    )(activations, targets, weight, e_all, b_all)
+    )(activations, targets, weight, e_all, b_all, *tail_in)
 
 
 def on_device(
@@ -389,10 +583,29 @@
         ],
         axis=0,
     )
+    tp_count = lax.axis_size("tp")
+    column_width = weight.shape[2]
+    if (
+        blocks == 1
+        and tp_count % 2 == 0
+        and column_width % (128 * tp_count) == 0
+        and units_here * CAP % 16 == 0
+    ):
+        coarse = gate_integer_weights // 256 * 256
+        fine = gate_integer_weights - coarse
+        gates = [
+            (jnp.sum(jnp.where(match, part[None], 0), axis=-1).T.astype(F32) / 65536.0).astype(BF16)
+            for part in (coarse, fine)
+        ]
+        mixed = routed_products(
+            activations, target, weight, mine, right_widening_matrices, ep_count, blocks,
+            [magnitude] + gates,
+        )
+        return mixed.reshape(tok_count, blocks, column_width // tp_count)
     partial_rows, squares = routed_products(
-        activations, target, weight, mine, right_widening_matrices, ep_count, blocks
+        activations, target, weight, mine, right_widening_matrices, ep_count, blocks, []
     )
-    total_sq = jnp.maximum(lax.psum(squares[:units_here], "tp"), 0.0)
+    total_sq = jnp.maximum(squares[:units_here], 0.0)
     col_scale = magnitude / jnp.sqrt(total_sq + 1e-06)
     gate_real = gate_integer_weights.astype(F32) / 65536.0
     combiner = jnp.sum(match.astype(F32) * gate_real[None, :, :], axis=-1).T

time: 217 us -> 102 us (0.47)
  Pallas kernels: 146 us -> 92.2 us
  waiting for transfers between devices: 30.9 us -> 0 us
  between operations: 13.5 us -> 0.11 us
  blocking collectives: 10.3 us -> 0 us
  starting transfers between devices: 4.62 us -> 0 us
    pallas_call x1, Pallas kernels: 146 us -> 92.2 us  [routed_products(): pl.pallas_call(functools.partial(dispatch_kernel, n, tp, units, blocks, r...]
    reduce_scatter x1 -> x0, waiting for transfers between devices: 17.1 us -> none  [on_device(): lax.psum_scatter(partial_rows, 'tp', scatter_dimension=1, tiled=True)]
    all_to_all x1 -> x0, waiting for transfers between devices: 13.7 us -> none  [on_device(): lax.all_to_all((summed * scale_part[None, :, None, :]).astype(BF16), 'ep'...]
    psum x1 -> x0, blocking collectives: 10.3 us -> none  [on_device(): total_sq = jnp.maximum(lax.psum(squares[:units_here], 'tp'), 0.0)]
    all_to_all x1 -> x0, starting transfers between devices: 4.62 us -> none  [on_device(): lax.all_to_all((summed * scale_part[None, :, None, :]).astype(BF16), 'ep'...]
  transfers between devices with their start and end apart: 2 -> 0, of which waited for: 2 -> 0; matrix products, arithmetic and copies ran while one was open for 1% -> 0% of each run, Pallas kernels for 0% -> 0%
where the time goes in v2:
time: 102 us
  Pallas kernels  92.2 us (90%)
  local copies, waits for them, and re-layouts  6.01 us (6%)
  other arithmetic  3.71 us (4%)
    pallas_call x1, Pallas kernels, routed_products(): pl.pallas_call(functools.partial(dispatch_kernel, n, tp, units, blocks, r...  92.2 us
    unnamed x4, local copies, waits for them, and re-layouts  2.49 us

profile of v2, /device:TPU:0, one launch (start us, length us, event | category | flops | bytes accessed | tf_op | source)
XLA Modules:
  0.0 102.1 jit_solution(1071496798344009684)
XLA Ops:
  0.0 1.0 constant_dynamic-slice_fusion.1
  1.0 0.1 copy.31
  1.1 0.1 copy.28
  1.2 0.4 mul.43
  1.6 0.4 mul.44
  2.0 0.1 mul.45
  2.2 0.8 broadcast_multiply_fusion.refs_3_
  3.0 0.8 copy.25
  3.8 0.1 eq.49
  3.9 0.6 reduce-window.6
  4.5 0.2 slice_reduce_fusion
  4.8 0.1 eq.45
  4.9 0.1 fusion.3
  5.0 0.1 reduce_sum.30
  5.2 0.1 copy.27
  5.2 0.7 fusion.6
  5.9 0.1 select_reduce_fusion
  6.0 0.1 copy.29
  6.2 0.7 fusion.refs_6_
  6.8 0.1 copy.30
  7.0 0.6 fusion.1.refs_7_
  7.6 0.6 pad.4.refs_1_
  8.2 92.2 %routed_products.1 = bf16[128,768]{1,0:T(8,128)(2,1)} custom-call(bf16[128,4096]{1,0:T(8,128)(2,1)} %refs_0_.1, s32[8,128]{1,0:T(8,128)} %pad.4.refs_1_, bf16[2,4096,3072]{2,1,0:T(8,128)(2,1)} %refs_2_.1, bf16[8,32,1024]{2,1,0:T(8,128)(2,1)} %broadcast_multiply_fusion.refs_3_, bf16[32,3072]{1,0:T(8,128)(2,1)} %bitcast.31, f32[2,3072]{1,0:T(2,128)} %refs_5_.1, ...), custom_call_target="tpu_custom_call" | custom-call | flops 8053063680 | bytes 50331648 | tf_op jit(solution)/shard_map/routed_products/pallas_call | solution.py:517
  100.4 1.6 %copy.34 = bf16[128,1,768]{2,0,1:T(8,128)(2,1)} copy(bf16[128,1,768]{2,0,1:T(8,128)(2,1)} %bitcast.28) | data formatting | bytes 393216
  (8 shorter events, 0.1 us)

commit v3 on v2

--- a/solution.py
+++ b/solution.py
@@ -8,8 +8,8 @@
 from jax.sharding import PartitionSpec as P
 
 CAP = 40
-KC = 512
-NB = 3
+KC = 1024
+NB = 2
 GAP = 1
 F32 = jnp.float32
 BF16 = jnp.bfloat16
@@ -478,7 +478,7 @@
     rp = -(-units * CAP // 16) * 16
     nc = feat // KC
     tp = lax.axis_size("tp")
-    tn = width // 3 if width % 384 == 0 else width
+    tn = width
     rows = n * rp
     low_t = mine.reshape(units, nc, KC, rank).transpose(1, 0, 3, 2)
     diag = jnp.eye(units, dtype=BF16)

time: 102 us -> 99.8 us (0.978)
  Pallas kernels: 92.2 us -> 89.8 us
    pallas_call x1, Pallas kernels: 92.2 us -> 89.8 us  [routed_products(): pl.pallas_call(functools.partial(dispatch_kernel, n, tp, units, blocks, r...]
    unnamed x4 -> x3, local copies, waits for them, and re-layouts: 2.49 us -> 2.43 us
where the time goes in v3:
time: 99.8 us; the launch traced here: 99.6 us
  Pallas kernels  89.8 us (90%)
  local copies, waits for them, and re-layouts  6.02 us (6%)
  other arithmetic  3.71 us (4%)
    pallas_call x1, Pallas kernels, routed_products(): pl.pallas_call(functools.partial(dispatch_kernel, n, tp, units, blocks, r...  89.8 us
    unnamed x3, local copies, waits for them, and re-layouts  2.43 us

profile of v3, /device:TPU:0, one launch (start us, length us, event | category | flops | bytes accessed | tf_op | source)
XLA Modules:
  0.0 99.6 jit_solution(15826771423397872165)
XLA Ops:
  0.0 1.0 constant_dynamic-slice_fusion.1
  1.0 0.2 reshape.50
  1.2 0.1 copy.28
  1.3 0.3 mul.43
  1.6 0.4 mul.44
  2.0 0.1 mul.45
  2.2 0.8 broadcast_multiply_fusion.refs_3_
  3.0 0.8 copy.25
  3.8 0.1 eq.49
  3.9 0.6 reduce-window.6
  4.5 0.2 slice_reduce_fusion
  4.8 0.1 eq.45
  4.9 0.1 fusion.3
  5.0 0.1 reduce_sum.30
  5.2 0.1 copy.27
  5.2 0.7 fusion.6
  5.9 0.1 select_reduce_fusion
  6.0 0.1 copy.29
  6.2 0.7 fusion.refs_6_
  6.8 0.1 copy.30
  7.0 0.6 fusion.1.refs_7_
  7.6 0.6 pad.4.refs_1_
  8.2 89.8 %routed_products.1 = bf16[128,768]{1,0:T(8,128)(2,1)} custom-call(bf16[128,4096]{1,0:T(8,128)(2,1)} %refs_0_.1, s32[8,128]{1,0:T(8,128)} %pad.4.refs_1_, bf16[2,4096,3072]{2,1,0:T(8,128)(2,1)} %refs_2_.1, bf16[4,32,2048]{2,1,0:T(8,128)(2,1)} %broadcast_multiply_fusion.refs_3_, bf16[32,3072]{1,0:T(8,128)(2,1)} %bitcast.25, f32[2,3072]{1,0:T(2,128)} %refs_5_.1, ...), custom_call_target="tpu_custom_call" | custom-call | flops 8053063680 | bytes 50331648 | tf_op jit(solution)/shard_map/routed_products/pallas_call | solution.py:517
  98.0 1.6 %copy.33 = bf16[128,1,768]{2,0,1:T(8,128)(2,1)} copy(bf16[128,1,768]{2,0,1:T(8,128)(2,1)} %bitcast.22) | data formatting | bytes 393216
  (8 shorter events, 0.1 us)
